TPU v7x, 32 devices: a whole 2x2x4 slice. The times are simulated.
32 devices in a mesh: seq: 8 (over z, y), head: 4 (over x, core).
Axes of the slice: x: 2, y: 2, z: 4, core: 2. Of those that a mesh axis runs over, the one named last changes fastest.
Arguments:
- queries: bfloat16 [1024, 32, 128], P('seq', 'head'), may hold values from -6 to 6
- keys: bfloat16 [1024, 2, 128], P('seq'), may hold values from -6 to 6
- values: bfloat16 [1024, 2, 128], P('seq'), may hold values from -6 to 6
- query_map: float32 [32, 128, 128], P('head'), may hold values from -0.5 to 0.5
- key_map: float32 [2, 128, 128], replicated, may hold values from -0.5 to 0.5
- window_logit: float32 [32], P('head'), may hold values from -2 to 2
Outputs:
- student: bfloat16 [1024, 32, 128], P('seq', 'head')
- teacher: bfloat16 [1024, 32, 128], P('seq', 'head')
- query_map_grad: float32 [32, 128, 128], P('head')
- key_map_grad: float32 [2, 128, 128], replicated
- window_grad: float32 [32], P('head')
All inputs are finite; a program needn't handle non-finite values.
Results may differ from a plain program's by a relative error of at most 0.0042.
Values may be sent and summed in bfloat16 or wider, within the bound.
A program may use at most 128 MiB of HBM per device.

v0:
```python
import jax
import jax.numpy as jnp
from jax import lax
from jax.sharding import PartitionSpec as P

GROUP_HEADS = 16
WINDOW = 64


PRECISE = lax.Precision.HIGHEST
NEGATIVE = -1e30


def shifted(value, axis, steps):
    count = lax.axis_size(axis)
    leading, last = (max(0, -steps), min(count, count - steps))
    return lax.ppermute(value, axis, [(source, source + steps) for source in range(leading, last)])


def prefix(value, axis, join, neutral):
    count, mine = (lax.axis_size(axis), lax.axis_index(axis))
    pieces = jax.tree.map(lambda part: lax.all_gather(part, axis), value)
    pieces = jax.tree.map(lambda part: part[::-1], pieces)
    mine = count - 1 - mine
    total = jax.tree.map(
        lambda part, zero: jnp.full_like(part, 0) + jnp.asarray(zero, part.dtype), value, neutral
    )

    def turn(position, total):
        longer = join(total, jax.tree.map(lambda part: part[position], pieces))
        return jax.tree.map(lambda new, old: jnp.where(position < mine, new, old), longer, total)

    return lax.fori_loop(0, count - 1, turn, total)


def hedgehog(preact):
    return jnp.concatenate(
        [jax.nn.softmax(preact, axis=-1), jax.nn.softmax(-preact, axis=-1)], axis=-1
    )


def add_pairs(first_pair, second_pair):
    return (first_pair[0] + second_pair[0], first_pair[1] + second_pair[1])


def shards(queries, keys, values, query_map, key_map, window_logit):
    tok_rows, heads_dev, head_width = queries.shape
    seq_count = lax.axis_size("seq")
    seq_index = lax.axis_index("seq")
    first_row = seq_index * tok_rows
    kv_group = lax.axis_index("head") * heads_dev // GROUP_HEADS
    own_keys = lax.dynamic_index_in_dim(keys, kv_group, 1, keepdims=False)
    own_values = lax.dynamic_index_in_dim(values, kv_group, 1, keepdims=False)
    own_map = lax.dynamic_index_in_dim(key_map, kv_group, 0, keepdims=False)
    score_scale = head_width ** (-0.5)
    query_pos = first_row + jnp.arange(tok_rows, dtype=jnp.int32)
    piece_keys = lax.all_gather(own_keys, "seq", axis=0, tiled=True)
    piece_values = lax.all_gather(own_values, "seq", axis=0, tiled=True)
    piece_rows = piece_keys.shape[0]
    row_peak = jnp.full((heads_dev, tok_rows), NEGATIVE, jnp.float32)
    scores = (
        jnp.einsum("thd,nd->htn", queries, piece_keys, preferred_element_type=jnp.float32)
        * score_scale
    )
    allowed = query_pos[:, None] >= jnp.arange(piece_rows, dtype=jnp.int32)[None, :]
    scores = jnp.where(allowed[None], scores, NEGATIVE)
    new_peak = jnp.maximum(row_peak, jnp.max(scores, axis=-1))
    weights = jnp.where(allowed[None], jnp.exp(scores - new_peak[..., None]), 0.0)
    weight_sum = jnp.sum(weights, axis=-1)
    weighted = jnp.einsum(
        "htn,nd->htd",
        weights.astype(jnp.bfloat16),
        piece_values,
        preferred_element_type=jnp.float32,
    )
    row_peak, weight_sum, weighted = (new_peak, weight_sum, weighted)
    teacher = (weighted / weight_sum[..., None]).astype(jnp.bfloat16)
    window = WINDOW
    rim_keys, rim_values = shifted(
        (own_keys[tok_rows - window :], own_values[tok_rows - window :]), "seq", 1
    )
    ext_keys = jnp.concatenate([rim_keys, own_keys], axis=0).astype(jnp.float32)
    ext_values = jnp.concatenate([rim_values, own_values], axis=0).astype(jnp.float32)
    ext_pos = first_row - window + jnp.arange(tok_rows + window, dtype=jnp.int32)
    present = ext_pos >= 0
    distance = query_pos[:, None] - ext_pos[None, :]
    near_mask = (distance >= 0) & (distance < window) & present[None, :]
    far_mask = ((distance >= window) & present[None, :]).astype(jnp.float32)
    query_f = queries.astype(jnp.float32)
    scores = jnp.einsum("thd,kd->htk", query_f, ext_keys, precision=PRECISE) * score_scale
    scores = jnp.where(near_mask[None], scores, NEGATIVE)
    window_weights = jnp.where(
        near_mask[None], jnp.exp(scores - jnp.max(scores, axis=-1, keepdims=True)), 0.0
    )
    window_mix = jnp.einsum("htk,kd->htd", window_weights, ext_values, precision=PRECISE)
    window_sum = jnp.sum(window_weights, axis=-1)

    def block_state(map_own):
        key_feats = hedgehog(jnp.dot(own_keys.astype(jnp.float32), map_own, precision=PRECISE))
        return (
            jnp.dot(key_feats.T, own_values.astype(jnp.float32), precision=PRECISE),
            jnp.sum(key_feats, axis=0),
        )

    (block_sum, state_norm), state_pull = jax.vjp(block_state, own_map)
    piece_sums = lax.all_gather(block_sum[None], "seq", axis=0, tiled=True)
    piece_norms = lax.all_gather(state_norm[None], "seq", axis=0, tiled=True)
    lower_mask = (jnp.arange(piece_sums.shape[0], dtype=jnp.int32) < seq_index).astype(jnp.float32)
    prior_state = jnp.einsum("n,nfd->fd", lower_mask, piece_sums, precision=PRECISE)
    prior_norm = jnp.einsum("n,nf->f", lower_mask, piece_norms, precision=PRECISE)

    def local_out(query_maps, map_own, logits, state_in, norm_in):
        query_feats = hedgehog(jnp.einsum("thd,hde->hte", query_f, query_maps, precision=PRECISE))
        key_feats = hedgehog(jnp.dot(ext_keys, map_own, precision=PRECISE))
        rim_feats = key_feats[:window] * present[:window, None].astype(jnp.float32)
        lin_state = state_in - jnp.dot(rim_feats.T, ext_values[:window], precision=PRECISE)
        lin_norm = norm_in - jnp.sum(rim_feats, axis=0)
        affinity = (
            jnp.einsum("htf,kf->htk", query_feats, key_feats, precision=PRECISE) * far_mask[None]
        )
        lin_mix = jnp.einsum("htk,kd->htd", affinity, ext_values, precision=PRECISE) + jnp.einsum(
            "htf,fd->htd", query_feats, lin_state, precision=PRECISE
        )
        lin_sum = jnp.sum(affinity, axis=-1) + jnp.einsum(
            "htf,f->ht", query_feats, lin_norm, precision=PRECISE
        )
        window_share = jax.nn.sigmoid(logits)[:, None]
        numerator = window_share[..., None] * window_mix + (1.0 - window_share[..., None]) * lin_mix
        denominator = window_share * window_sum + (1.0 - window_share) * lin_sum
        return numerator / denominator[..., None]

    student_f, out_pull = jax.vjp(
        local_out, query_map, own_map, window_logit, prior_state, prior_norm
    )
    length_all = tok_rows * seq_count
    residual_grad = (student_f - teacher.astype(jnp.float32)) / length_all
    query_grad, key_grad_local, logit_grad, state_grad, norm_grad = out_pull(residual_grad)
    later_state, later_norm = prefix(
        (state_grad, norm_grad),
        "seq",
        add_pairs,
        (jnp.zeros_like(state_grad), jnp.zeros_like(norm_grad)),
    )
    (key_grad_chain,) = state_pull((later_state, later_norm))
    key_slot = (jnp.arange(key_map.shape[0], dtype=jnp.int32) == kv_group).astype(jnp.float32)
    slotted = key_slot[:, None, None] * (key_grad_local + key_grad_chain)[None]
    query_grad, logit_grad = lax.psum((query_grad, logit_grad), "seq")
    key_grad_total = lax.psum(slotted, ("seq", "head"))
    student_out = jnp.transpose(student_f, (1, 0, 2)).astype(jnp.bfloat16)
    teacher_out = jnp.transpose(teacher, (1, 0, 2))
    return (student_out, teacher_out, query_grad, key_grad_total, logit_grad)


def solution(mesh):
    placed = (
        P("seq", "head", None),
        P("seq", None, None),
        P("seq", None, None),
        P("head", None, None),
        P(),
        P("head"),
    )
    return jax.shard_map(
        shards,
        mesh=mesh,
        in_specs=placed,
        out_specs=(
            P("seq", "head", None),
            P("seq", "head", None),
            P("head", None, None),
            P(),
            P("head"),
        ),
        check_vma=False,
    )
```

profile of v0, /device:TPU:0, one launch (start us, length us, event | category | flops | bytes accessed | tf_op | source)
XLA Modules:
  0.0 377.0 jit_solution(6598448560078703371)
XLA Ops:
  7.3 1.0 constant_dynamic-slice_fusion.2
  8.3 4.9 %collective-permute-start = (bf16[64,128]{1,0:T(8,128)(2,1)S(1)}, bf16[64,128]{1,0:T(8,128)(2,1)S(1)}, u32[]{:S(2)}, u32[]{:S(2)}) collective-permute-start(bf16[64,128]{1,0:T(8,128)(2,1)S(1)} %slice_bitcast_fusion.1), channel_id=1, source_target_pairs={{0,4},{4,8},{8,12},{12,16},{16,20},{20,24},{24,28},{1,5},{5,9},{9,... | collective-permute-start | bytes 49160 | tf_op jit(solution)/shard_map/ppermute | solution.py:17
  13.2 0.9 constant_dynamic-slice_fusion.1
  14.1 3.4 collective-permute-start.1
  17.5 1.1 fusion.151
  18.7 0.5 copy-done.11
  19.3 0.9 fusion.63
  20.3 31.1 %all-gather.2 = bf16[1024,1,128]{2,0,1:T(8,128)(2,1)S(1)} all-gather(bf16[128,1,128]{2,0,1:T(8,128)(2,1)S(1)} %copy.76), channel_id=4, replica_groups=mesh['seq'=8,'head'=4] {'seq'}, dimensions={0}, use_global_device_ids=true | all-gather | bytes 294912 | tf_op jit(solution)/shard_map/all_gather | solution.py:57
  51.4 30.9 %all-gather.3 = bf16[1024,1,128]{2,0,1:T(8,128)(2,1)S(1)} all-gather(bf16[128,1,128]{2,0,1:T(8,128)(2,1)S(1)} %copy.77), channel_id=5, replica_groups=mesh['seq'=8,'head'=4] {'seq'}, dimensions={0}, use_global_device_ids=true | all-gather | bytes 294912 | tf_op jit(solution)/shard_map/all_gather | solution.py:58
  82.3 1.6 fusion.53
  83.8 0.5 fusion.152
  84.3 0.5 fusion.153
  84.9 0.6 multiply_divide_fusion.5
  85.8 0.7 fusion.2
  86.7 18.2 %all-gather.6 = f32[8,1,256]{2,1,0:T(1,128)S(1)} all-gather(f32[1,1,256]{2,1,0:T(1,128)S(1)} %bitcast.162), channel_id=3, replica_groups=mesh['seq'=8,'head'=4] {'seq'}, dimensions={0}, use_global_device_ids=true | all-gather | bytes 9216 | tf_op jit(solution)/shard_map/all_gather | solution.py:107
  105.0 1.0 fusion.3
  106.1 1.9 fusion.21
  108.0 0.6 multiply_divide_fusion.1
  108.7 0.5 compare_convert_fusion
  109.3 0.9 copy.53
  111.6 0.6 fusion.60
  112.3 1.8 fusion.155
  114.2 0.5 multiply_divide_fusion.3
  114.7 1.4 fusion.20
  116.1 2.4 fusion.17
  118.9 0.7 fusion.61
  119.7 2.8 multiply_reduce_fusion.1
  122.5 1.7 convolution_bitcast_fusion.2
  124.2 1.2 multiply_reduce_fusion.4
  125.4 0.7 multiply_reduce_fusion.10
  126.1 2.1 convolution_add_fusion.1
  128.6 1.5 fusion.10
  130.1 2.4 convolution_add_fusion
  132.6 1.0 copy-done.3
  133.6 1.2 multiply_reduce_fusion.3
  134.8 0.6 neg.90
  135.4 0.6 neg.88
  136.0 0.9 fusion.59
  136.9 16.5 %all-gather.7 = f32[8,1,256]{2,1,0:T(1,128)S(1)} all-gather(f32[1,1,256]{2,1,0:T(1,128)S(1)} %bitcast.159), channel_id=7, replica_groups=mesh['seq'=8,'head'=4] {'seq'}, dimensions={0}, use_global_device_ids=true | all-gather | bytes 9216 | tf_op jit(solution)/shard_map/all_gather | solution.py:22
  153.4 0.6 copy.99
  154.0 1.3 rev.7
  155.3 0.7 neg.91
  155.9 1.1 fusion.16
  157.1 1.2 pad_add_fusion
  158.3 1.3 multiply_reduce_fusion.6
  159.7 2.6 convolution_bitcast_fusion
  162.6 3.1 all-gather.13.cloned.1.call-done
  165.7 1.3 rev.6
  167.0 5.5 %while.16 = (s32[]{:T(128)}, f32[256,128]{1,0:T(8,128)S(1)}, f32[256]{0:T(256)S(1)}, s32[]{:T(128)}, f32[8,256,128]{2,1,0:T(8,128)S(1)}, /*index=5*/f32[8,256]{1,0:T(8,128)}, s32[]{:T(128)}, s32[]{:T(128)}) while((s32[]{:T(128)}, f32[256,128]{1,0:T(8,128)S(1)}, f32[256]{0:T(256)S(1)}, s32[]{:T(128)}, ...), condition=%wide.region_26.27_spmd.clone, body=%wide.region_25.26_spmd.clone.sunk | while | flops 99076 | bytes 398459 | solution.py:33
  167.1 0.7 constant_dynamic-slice_fusion.4
  167.8 0.7 constant_dynamic-slice_fusion.4
  168.6 0.7 constant_dynamic-slice_fusion.4
  169.4 0.7 constant_dynamic-slice_fusion.4
  170.2 0.7 constant_dynamic-slice_fusion.4
  171.0 0.7 constant_dynamic-slice_fusion.4
  171.8 0.7 constant_dynamic-slice_fusion.4
  173.2 0.5 convolution_add_fusion.5
  173.7 0.7 broadcast_multiply_fusion
  174.5 19.8 %psum.23 = f32[8]{0:T(128)} all-reduce(f32[8]{0:T(128)S(1)} %multiply_multiply_fusion), channel_id=1, replica_groups=mesh['seq'=8,'head'=4] {'seq'}, use_global_device_ids=true, to_apply=%region_34.35 | all-reduce | flops 8 | bytes 64 | tf_op jit(solution)/shard_map/psum | solution.py:147
  194.3 0.9 copy.52
  195.2 45.0 %all-reduce.4.cloned.1.call-done = f32[8,128,128]{1,2,0:T(8,128)} async-done(((f32[8,128,128]{1,2,0:T(8,128)}), f32[8,128,128]{1,2,0:T(8,128)}) %all-reduce.4.cloned.1.call-update) | async-done | bytes 524304 | tf_op jit(solution)/shard_map/psum | solution.py:147
  240.2 2.0 copy.54
  242.2 126.6 %all-reduce.6.cloned.1.call-done = f32[2,128,128]{2,1,0:T(8,128)} async-done(((f32[2,128,128]{2,1,0:T(8,128)}), f32[2,128,128]{2,1,0:T(8,128)}) %all-reduce.6.cloned.1.call-update) | async-done | bytes 131088 | tf_op jit(solution)/shard_map/psum | solution.py:148
  368.9 1.6 copy.113
  (186 shorter events, 4.1 us)
Async XLA Ops:
  7.2 75.1 %copy-start = (f32[8,128,128]{2,1,0:T(8,128)S(1)}, f32[8,128,128]{2,1,0:T(8,128)}, u32[]{:S(2)}) copy-start(f32[8,128,128]{2,1,0:T(8,128)} %param.11) | copy-start | bytes 1572868
  7.2 78.6 %copy-start.6 = (bf16[128,8,128]{2,1,0:T(8,128)(2,1)S(1)}, bf16[128,8,128]{2,1,0:T(8,128)(2,1)}, u32[]{:S(2)}) copy-start(bf16[128,8,128]{2,1,0:T(8,128)(2,1)} %param.8) | copy-start | bytes 786436
  7.2 108.9 %all-gather.11.cloned.1.call-start = ((), (), s32[]{:S(2)}) async-start(), calls=%async_computation.2 | async-start | bytes 1179648 | tf_op jit(solution)/shard_map/all_gather | solution.py:106
  8.2 78.3 %copy-start.18 = (bf16[128,1,128]{2,0,1:T(8,128)(2,1)}, bf16[128,1,128]{2,0,1:T(8,128)(2,1)S(1)}, u32[]{:S(2)}) copy-start(bf16[128,1,128]{2,0,1:T(8,128)(2,1)S(1)} %copy.76) | copy-start | bytes 98308
  8.3 101.9 %collective-permute-start = (bf16[64,128]{1,0:T(8,128)(2,1)S(1)}, bf16[64,128]{1,0:T(8,128)(2,1)S(1)}, u32[]{:S(2)}, u32[]{:S(2)}) collective-permute-start(bf16[64,128]{1,0:T(8,128)(2,1)S(1)} %slice_bitcast_fusion.1), channel_id=1, source_target_pairs={{0,4},{4,8},{8,12},{12,16},{16,20},{20,24},{24,28},{1,5},{5,9},{9,... | collective-permute-start | bytes 49160 | tf_op jit(solution)/shard_map/ppermute | solution.py:17
  14.1 72.5 %copy-start.16 = (bf16[128,1,128]{2,0,1:T(8,128)(2,1)}, bf16[128,1,128]{2,0,1:T(8,128)(2,1)S(1)}, u32[]{:S(2)}) copy-start(bf16[128,1,128]{2,0,1:T(8,128)(2,1)S(1)} %copy.77) | copy-start | bytes 98308
  14.1 100.6 %collective-permute-start.1 = (bf16[64,128]{1,0:T(8,128)(2,1)S(1)}, bf16[64,128]{1,0:T(8,128)(2,1)S(1)}, u32[]{:S(2)}, u32[]{:S(2)}) collective-permute-start(bf16[64,128]{1,0:T(8,128)(2,1)S(1)} %slice_bitcast_fusion), channel_id=1, source_target_pairs={{0,4},{4,8},{8,12},{12,16},{16,20},{20,24},{24,28},{1,5},{5,9},{9,... | collective-permute-start | bytes 49160 | tf_op jit(solution)/shard_map/ppermute | solution.py:17
  18.7 67.0 %copy-start.43 = (f32[128]{0:T(128)}, f32[128]{0:T(128)S(1)}, u32[]{:S(2)}) copy-start(f32[128]{0:T(128)S(1)} %get-tuple-element.162) | copy-start | bytes 1540
  18.7 67.9 %copy-start.45 = (f32[128]{0:T(128)}, f32[128]{0:T(128)S(1)}, u32[]{:S(2)}) copy-start(f32[128]{0:T(128)S(1)} %get-tuple-element.163) | copy-start | bytes 1540
  18.7 67.9 %copy-start.48 = (f32[128]{0:T(128)}, f32[128]{0:T(128)S(1)}, u32[]{:S(2)}) copy-start(f32[128]{0:T(128)S(1)} %get-tuple-element.160) | copy-start | bytes 1540
  18.7 67.9 %copy-start.50 = (f32[128]{0:T(128)}, f32[128]{0:T(128)S(1)}, u32[]{:S(2)}) copy-start(f32[128]{0:T(128)S(1)} %get-tuple-element.161) | copy-start | bytes 1540
  20.2 145.5 %all-gather.13.cloned.1.call-start = ((), (), s32[]{:S(2)}) async-start(), calls=%async_computation.3 | async-start | bytes 1179648 | tf_op jit(solution)/shard_map/all_gather | solution.py:22
  82.3 4.3 %copy-start.61 = (f32[8]{0:T(128)S(1)}, f32[8]{0:T(128)}, u32[]{:S(2)}) copy-start(f32[8]{0:T(128)} %param.13) | copy-start | bytes 100
  84.3 24.3 %copy-start.30 = (f32[8,128]{1,0:T(8,128)}, f32[8,128]{1,0:T(8,128)S(1)}, u32[]{:S(2)}) copy-start(f32[8,128]{1,0:T(8,128)S(1)} %get-tuple-element.194) | copy-start | bytes 12292
  84.8 23.8 %copy-start.1 = (f32[8,128,128]{1,2,0:T(8,128)}, f32[8,128,128]{1,2,0:T(8,128)S(1)}, u32[]{:S(2)}) copy-start(f32[8,128,128]{1,2,0:T(8,128)S(1)} %get-tuple-element.197) | copy-start | bytes 1572868
  84.8 23.8 %copy-start.31 = (f32[8,128]{1,0:T(8,128)}, f32[8,128]{1,0:T(8,128)S(1)}, u32[]{:S(2)}) copy-start(f32[8,128]{1,0:T(8,128)S(1)} %get-tuple-element.196) | copy-start | bytes 12292
  85.6 32.9 %copy-start.47 = (f32[64]{0:T(128)}, f32[64]{0:T(128)S(1)}, u32[]{:S(2)}) copy-start(f32[64]{0:T(128)S(1)} %slice_convert_fusion) | copy-start | bytes 772
  85.8 26.5 %copy-start.13 = (f32[128,192]{0,1:T(8,128)}, f32[128,192]{0,1:T(8,128)S(1)}, u32[]{:S(2)}) copy-start(f32[128,192]{0,1:T(8,128)S(1)} %get-tuple-element.191) | copy-start | bytes 294916
  86.6 33.1 %copy-start.54 = (f32[8]{0:T(128)}, f32[8]{0:T(128)S(1)}, u32[]{:S(2)}) copy-start(f32[8]{0:T(128)S(1)} %get-tuple-element.184) | copy-start | bytes 100
  86.6 39.5 %copy-start.37 = (f32[8]{0:T(128)}, f32[8]{0:T(128)S(1)}, u32[]{:S(2)}) copy-start(f32[8]{0:T(128)S(1)} %get-tuple-element.183) | copy-start | bytes 100
  106.0 4.1 %copy-start.23 = (f32[2,128,128]{2,1,0:T(8,128)S(1)}, f32[2,128,128]{2,1,0:T(8,128)}, u32[]{:S(2)}) copy-start(f32[2,128,128]{2,1,0:T(8,128)} %param.12) | copy-start | bytes 393220
  109.2 9.3 %copy-start.21 = (bf16[128,1,128]{2,0,1:T(8,128)(2,1)}, bf16[128,1,128]{2,0,1:T(8,128)(2,1)S(1)}, u32[]{:S(2)}) copy-start(bf16[128,1,128]{2,0,1:T(8,128)(2,1)S(1)} %copy.101) | copy-start | bytes 98308
  109.3 10.4 %copy-start.20 = (bf16[128,1,128]{2,0,1:T(8,128)(2,1)}, bf16[128,1,128]{2,0,1:T(8,128)(2,1)S(1)}, u32[]{:S(2)}) copy-start(bf16[128,1,128]{2,0,1:T(8,128)(2,1)S(1)} %copy.100) | copy-start | bytes 98308
  110.2 8.3 %copy-start.26 = (bf16[64,128]{1,0:T(8,128)(2,1)}, bf16[64,128]{1,0:T(8,128)(2,1)S(1)}, u32[]{:S(2)}) copy-start(bf16[64,128]{1,0:T(8,128)(2,1)S(1)} %collective-permute-done) | copy-start | bytes 49156
  110.5 3.6 copy-start.35
  110.8 8.1 %copy-start.38 = (f32[192]{0:T(256)}, f32[192]{0:T(256)S(1)}, u32[]{:S(2)}) copy-start(f32[192]{0:T(256)S(1)} %get-tuple-element.156) | copy-start | bytes 2308
  110.8 8.1 %copy-start.40 = (f32[192]{0:T(256)}, f32[192]{0:T(256)S(1)}, u32[]{:S(2)}) copy-start(f32[192]{0:T(256)S(1)} %get-tuple-element.157) | copy-start | bytes 2308
  111.0 7.9 %copy-start.4 = (f32[192,128]{1,0:T(8,128)}, f32[192,128]{1,0:T(8,128)S(1)}, u32[]{:S(2)}) copy-start(f32[192,128]{1,0:T(8,128)S(1)} %get-tuple-element.185) | copy-start | bytes 294916
  111.0 7.9 %copy-start.5 = (f32[192,128]{1,0:T(8,128)}, f32[192,128]{1,0:T(8,128)S(1)}, u32[]{:S(2)}) copy-start(f32[192,128]{1,0:T(8,128)S(1)} %get-tuple-element.186) | copy-start | bytes 294916
  114.2 10.0 %copy-start.28 = (f32[8,128]{1,0:T(8,128)}, f32[8,128]{1,0:T(8,128)S(1)}, u32[]{:S(2)}) copy-start(f32[8,128]{1,0:T(8,128)S(1)} %get-tuple-element.181) | copy-start | bytes 12292
  122.5 5.8 %copy-start.7 = (f32[8,128,128]{1,2,0:T(8,128)}, f32[8,128,128]{1,2,0:T(8,128)S(1)}, u32[]{:S(2)}) copy-start(f32[8,128,128]{1,2,0:T(8,128)S(1)} %get-tuple-element.179) | copy-start | bytes 1572868
  126.1 2.2 copy-start.24
  128.3 111.9 %all-reduce.4.cloned.1.call-start = ((), (), s32[]{:S(2)}) async-start(), calls=%async_computation | async-start | bytes 1048576 | tf_op jit(solution)/shard_map/psum | solution.py:147
  128.6 7.4 %copy-start.25 = (f32[8,128]{1,0:T(8,128)S(1)}, f32[8,128]{1,0:T(8,128)}, u32[]{:S(2)}) copy-start(f32[8,128]{1,0:T(8,128)} %copy-done.24) | copy-start | bytes 12292
  130.1 29.5 %copy-start.2 = (f32[8,128,128]{1,2,0:T(8,128)S(1)}, f32[8,128,128]{1,2,0:T(8,128)}, u32[]{:S(2)}) copy-start(f32[8,128,128]{1,2,0:T(8,128)} %copy-done.1) | copy-start | bytes 1572868
  136.9 17.1 %copy-start.42 = (f32[1,256,1]{1,0,2:T(1,128)}, f32[1,256,1]{1,0,2:T(1,128)S(1)}, u32[]{:S(2)}) copy-start(f32[1,256,1]{1,0,2:T(1,128)S(1)} %fusion.59) | copy-start | bytes 3076
  157.1 5.4 %copy-start.55 = (f32[8]{0:T(128)S(1)}, f32[8]{0:T(128)}, u32[]{:S(2)}) copy-start(f32[8]{0:T(128)} %copy-done.54) | copy-start | bytes 100
  157.1 5.4 %copy-start.56 = (f32[8]{0:T(128)S(1)}, f32[8]{0:T(128)}, u32[]{:S(2)}) copy-start(f32[8]{0:T(128)} %get-tuple-element.164) | copy-start | bytes 100
  157.1 5.4 %copy-start.57 = (f32[8]{0:T(128)S(1)}, f32[8]{0:T(128)}, u32[]{:S(2)}) copy-start(f32[8]{0:T(128)} %get-tuple-element.165) | copy-start | bytes 100
  157.1 5.4 %copy-start.59 = (f32[8]{0:T(128)S(1)}, f32[8]{0:T(128)}, u32[]{:S(2)}) copy-start(f32[8]{0:T(128)} %get-tuple-element.150) | copy-start | bytes 100
  158.3 1.3 copy-start.14
  158.3 4.2 %copy-start.60 = (f32[8]{0:T(128)S(1)}, f32[8]{0:T(128)}, u32[]{:S(2)}) copy-start(f32[8]{0:T(128)} %get-tuple-element.151) | copy-start | bytes 100
  158.3 8.7 %copy-start.32 = (f32[256]{0:T(256)S(1)}, f32[256]{0:T(256)}, u32[]{:S(2)}) copy-start(f32[256]{0:T(256)} %custom-call.1) | copy-start | bytes 3076
  159.6 12.8 %copy-start.17 = (bf16[128,1,128]{2,0,1:T(8,128)(2,1)S(1)}, bf16[128,1,128]{2,0,1:T(8,128)(2,1)}, u32[]{:S(2)}) copy-start(bf16[128,1,128]{2,0,1:T(8,128)(2,1)} %copy-done.16) | copy-start | bytes 98308
  159.6 13.1 %copy-start.12 = (f32[128,128]{0,1:T(8,128)S(1)}, f32[128,128]{0,1:T(8,128)}, u32[]{:S(2)}) copy-start(f32[128,128]{0,1:T(8,128)} %copy-done.11) | copy-start | bytes 196612
  159.7 13.1 %copy-start.44 = (f32[128]{0:T(128)S(1)}, f32[128]{0:T(128)}, u32[]{:S(2)}) copy-start(f32[128]{0:T(128)} %copy-done.43) | copy-start | bytes 1540
  159.7 13.1 %copy-start.46 = (f32[128]{0:T(128)S(1)}, f32[128]{0:T(128)}, u32[]{:S(2)}) copy-start(f32[128]{0:T(128)} %copy-done.45) | copy-start | bytes 1540
  159.7 13.1 %copy-start.52 = (f32[128]{0:T(128)S(1)}, f32[128]{0:T(128)}, u32[]{:S(2)}) copy-start(f32[128]{0:T(128)} %get-tuple-element.210) | copy-start | bytes 1540
  159.7 13.1 %copy-start.53 = (f32[128]{0:T(128)S(1)}, f32[128]{0:T(128)}, u32[]{:S(2)}) copy-start(f32[128]{0:T(128)} %get-tuple-element.211) | copy-start | bytes 1540
  159.7 13.2 %copy-start.19 = (bf16[128,1,128]{2,0,1:T(8,128)(2,1)S(1)}, bf16[128,1,128]{2,0,1:T(8,128)(2,1)}, u32[]{:S(2)}) copy-start(bf16[128,1,128]{2,0,1:T(8,128)(2,1)} %copy-done.18) | copy-start | bytes 98308
  159.7 13.2 %copy-start.49 = (f32[128]{0:T(128)S(1)}, f32[128]{0:T(128)}, u32[]{:S(2)}) copy-start(f32[128]{0:T(128)} %copy-done.48) | copy-start | bytes 1540
  159.7 13.2 %copy-start.51 = (f32[128]{0:T(128)S(1)}, f32[128]{0:T(128)}, u32[]{:S(2)}) copy-start(f32[128]{0:T(128)} %copy-done.50) | copy-start | bytes 1540
  162.3 10.8 %copy-start.10 = (f32[192,128]{1,0:T(8,128)S(1)}, f32[192,128]{1,0:T(8,128)}, u32[]{:S(2)}) copy-start(f32[192,128]{1,0:T(8,128)} %copy-done.9) | copy-start | bytes 294916
  162.3 10.8 %copy-start.15 = (f32[192,256]{1,0:T(8,128)S(1)}, f32[192,256]{1,0:T(8,128)}, u32[]{:S(2)}) copy-start(f32[192,256]{1,0:T(8,128)} %copy-done.14) | copy-start | bytes 589828
  162.3 10.8 %copy-start.22 = (bf16[128,1,128]{2,0,1:T(8,128)(2,1)S(1)}, bf16[128,1,128]{2,0,1:T(8,128)(2,1)}, u32[]{:S(2)}) copy-start(bf16[128,1,128]{2,0,1:T(8,128)(2,1)} %copy-done.21) | copy-start | bytes 98308
  162.3 10.8 %copy-start.27 = (bf16[64,128]{1,0:T(8,128)(2,1)S(1)}, bf16[64,128]{1,0:T(8,128)(2,1)}, u32[]{:S(2)}) copy-start(bf16[64,128]{1,0:T(8,128)(2,1)} %copy-done.26) | copy-start | bytes 49156
  162.3 10.8 %copy-start.34 = (f32[192]{0:T(256)S(1)}, f32[192]{0:T(256)}, u32[]{:S(2)}) copy-start(f32[192]{0:T(256)} %copy-done.33) | copy-start | bytes 2308
  162.4 10.8 %copy-start.36 = (f32[192]{0:T(256)S(1)}, f32[192]{0:T(256)}, u32[]{:S(2)}) copy-start(f32[192]{0:T(256)} %copy-done.35) | copy-start | bytes 2308
  162.4 10.8 %copy-start.39 = (f32[192]{0:T(256)S(1)}, f32[192]{0:T(256)}, u32[]{:S(2)}) copy-start(f32[192]{0:T(256)} %copy-done.38) | copy-start | bytes 2308
  162.4 10.8 %copy-start.41 = (f32[192]{0:T(256)S(1)}, f32[192]{0:T(256)}, u32[]{:S(2)}) copy-start(f32[192]{0:T(256)} %copy-done.40) | copy-start | bytes 2308
  162.4 11.3 %copy-start.58 = (f32[2]{0:T(128)S(1)}, f32[2]{0:T(128)}, u32[]{:S(2)}) copy-start(f32[2]{0:T(128)} %compare_convert_fusion) | copy-start | bytes 28
  162.4 12.0 %copy-start.8 = (f32[8,128,128]{1,2,0:T(8,128)S(1)}, f32[8,128,128]{1,2,0:T(8,128)}, u32[]{:S(2)}) copy-start(f32[8,128,128]{1,2,0:T(8,128)} %copy-done.7) | copy-start | bytes 1572868
  162.4 12.0 %copy-start.29 = (f32[8,128]{1,0:T(8,128)S(1)}, f32[8,128]{1,0:T(8,128)}, u32[]{:S(2)}) copy-start(f32[8,128]{1,0:T(8,128)} %copy-done.28) | copy-start | bytes 12292
  162.4 206.4 %all-reduce.6.cloned.1.call-start = ((), (), s32[]{:S(2)}) async-start(), calls=%async_computation.1 | async-start | bytes 262144 | tf_op jit(solution)/shard_map/psum | solution.py:148
  (4 other events, 2.9 us)
Sparse Core Ops, SparseCore 0:
  20.3 41.5 all-gather.10
  128.4 37.2 all-gather.12
  169.1 71.0 all-reduce.3
  247.1 121.7 all-reduce.5
where the time goes:
time: 378 us; the launch traced here: 377 us
  waiting for transfers between devices  175 us (46%)
  blocking collectives  116 us (31%)
  matrix products  31.6 us (8%)
  local copies, waits for them, and re-layouts  17.3 us (5%)
  between operations  14.9 us (4%)
  other arithmetic  13 us (3%)
  starting transfers between devices  8.68 us (2%)
    psum x1, waiting for transfers between devices, shards(): key_grad_total = lax.psum(slotted, ('seq', 'head'))  127 us
    psum x1, waiting for transfers between devices, shards(): query_grad, logit_grad = lax.psum((query_grad, logit_grad), 'seq')  45 us
    all_gather x1, blocking collectives, shards(): piece_keys = lax.all_gather(own_keys, 'seq', axis=0, tiled=True)  31.1 us
    all_gather x1, blocking collectives, shards(): piece_values = lax.all_gather(own_values, 'seq', axis=0, tiled=True)  30.9 us
    psum x1, blocking collectives, shards(): query_grad, logit_grad = lax.psum((query_grad, logit_grad), 'seq')  19.8 us
    all_gather x1, blocking collectives, shards(): piece_norms = lax.all_gather(state_norm[None], 'seq', axis=0, tiled=True)  18.2 us
    all_gather x1, blocking collectives, prefix(): pieces = jax.tree.map(lambda part: lax.all_gather(part, axis), value)  16.5 us
    ppermute x2, starting transfers between devices, shifted(): lax.ppermute(value, axis, [(source, source + steps) for source in range(l...  8.3 us
  transfers between devices with their start and end apart: 6, of which 3 were waited for; matrix products, arithmetic and copies ran while one was open for 12% of the time, Pallas kernels for 0%

commit v1 on v0

v1 whole, which is shorter than its diff:
```python
import functools

import jax
import jax.numpy as jnp
from jax import lax
from jax.experimental import pallas as pl
from jax.experimental.pallas import tpu as pltpu
from jax.sharding import PartitionSpec as P

GROUP_HEADS = 16
WINDOW = 64
NEGATIVE = -1e30
F32 = jnp.float32
BF16 = jnp.bfloat16
NN = (((1,), (0,)), ((), ()))
NT = (((1,), (1,)), ((), ()))
TN = (((0,), (0,)), ((), ()))


def mm(a, b, dims):
    return lax.dot_general(a.astype(BF16), b.astype(BF16), dims, preferred_element_type=F32)


def split(x):
    high = x.astype(BF16)
    return high, (x - high.astype(F32)).astype(BF16)


def mm_lhs(x, b, dims):
    high, low = split(x)
    return mm(high, b, dims) + mm(low, b, dims)


def mm_rhs(a, x, dims):
    high, low = split(x)
    return mm(a, high, dims) + mm(a, low, dims)


def soft(x):
    e = jnp.exp(x - jnp.max(x, axis=-1, keepdims=True))
    return e / jnp.sum(e, axis=-1, keepdims=True)


def feature_pull(p, n, dp, dn):
    return p * (dp - jnp.sum(p * dp, axis=-1, keepdims=True)) - n * (
        dn - jnp.sum(n * dn, axis=-1, keepdims=True)
    )


def with_ones(v):
    ones = (lax.broadcasted_iota(jnp.int32, v.shape, 1) == 0).astype(F32).astype(v.dtype)
    return jnp.concatenate([v, ones], axis=1)


def iota(shape, dim):
    return lax.broadcasted_iota(jnp.int32, shape, dim)


def local_kernel(
    sizes, q_ref, kv_ref, mq_ref, mk_ref, logit_ref,
    student_ref, teacher_ref, qgrad_ref, kgrad_ref, lgrad_ref,
    q_scr, out_scr, tea_scr, feat, state, dstate, dext, kpad, vpad, high, low,
):
    count, tok, heads, width, chunk = sizes
    length = count * tok
    scale = width ** (-0.5)
    seq = lax.axis_index("seq")
    first = pl.multiple_of(seq * tok, tok)
    group = lax.axis_index("head") * heads // GROUP_HEADS
    q_scr[...] = q_ref[...].astype(F32).reshape(tok * heads, width)
    kpad[:WINDOW] = jnp.zeros((WINDOW, width), BF16)
    vpad[:WINDOW] = jnp.zeros((WINDOW, width), BF16)
    feat[:WINDOW] = jnp.zeros((WINDOW, 2 * width), F32)
    kpad[WINDOW:] = kv_ref[:, 0].reshape(length, width)
    vpad[WINDOW:] = kv_ref[:, 1].reshape(length, width)
    state[...] = jnp.zeros_like(state)
    dstate[...] = jnp.zeros_like(dstate)
    dext[...] = jnp.zeros_like(dext)
    map_own = mk_ref[group]

    @pl.loop(0, length // chunk)
    def _(c):
        begin = pl.multiple_of(c * chunk, chunk)
        rows = pl.ds(WINDOW + begin, chunk)
        pre = mm_rhs(kpad[rows], map_own, NN)
        kf = jnp.concatenate([soft(pre), soft(-pre)], axis=1)
        feat[rows] = kf
        before = (begin + iota((chunk, 1), 0)) < first - WINDOW
        state[...] += mm(jnp.where(before, kf, 0.0), with_ones(vpad[rows]), TN)

    state_high, state_low = split(state[...])
    high[...] = state_high
    low[...] = state_low
    near = pl.ds(first, tok)
    ext = pl.ds(first, tok + WINDOW)

    @pl.loop(0, heads)
    def _(h):
        mine = pl.ds(h, tok, stride=heads)
        qf32 = q_scr[mine, :]
        q = qf32.astype(BF16)
        scores = mm(q, kpad[WINDOW:], NT) * scale
        seen = first + iota((tok, 1), 0) >= iota((1, length), 1)
        scores = jnp.where(seen, scores, NEGATIVE)
        weights = jnp.exp(scores - jnp.max(scores, axis=-1, keepdims=True))
        total = jnp.sum(weights, axis=-1, keepdims=True)
        teacher = (mm(weights, vpad[WINDOW:], NN) / total).astype(BF16).astype(F32)
        tea_scr[mine, :] = teacher
        sw = mm(q, kpad[ext], NT) * scale
        row, col = iota((tok, tok + WINDOW), 0), iota((tok, tok + WINDOW), 1)
        inside = (col > row) & (col <= row + WINDOW) & (first - WINDOW + col >= 0)
        sw = jnp.where(inside, sw, NEGATIVE)
        ww = jnp.where(inside, jnp.exp(sw - jnp.max(sw, axis=-1, keepdims=True)), 0.0)
        window_sum = jnp.sum(ww, axis=-1, keepdims=True)
        window_mix = mm_lhs(ww, vpad[ext], NN)
        pre = mm_rhs(q, mq_ref[h], NN)
        p, n = soft(pre), soft(-pre)
        qf = jnp.concatenate([p, n], axis=1)
        kf = feat[near].astype(BF16)
        v_near = with_ones(vpad[near])
        far = iota((tok, tok), 0) >= iota((tok, tok), 1)
        aff = jnp.where(far, mm(qf, kf, NT), 0.0)
        lin = mm_lhs(aff, v_near, NN) + mm(qf, high[...], NN) + mm(qf, low[...], NN)
        lin_mix, lin_sum = lin[:, :width], lin[:, width : width + 1]
        share = jax.nn.sigmoid(jnp.full((1, 1), logit_ref[h], F32))
        rest = 1.0 - share
        den = share * window_sum + rest * lin_sum
        out = (share * window_mix + rest * lin_mix) / den
        out_scr[mine, :] = out
        a = (out - teacher) * (1.0 / length) / den
        c = jnp.sum(a * out, axis=-1, keepdims=True)
        dshare = jnp.sum(a * (window_mix - lin_mix), axis=-1, keepdims=True) - c * (
            window_sum - lin_sum
        )
        lgrad_ref[pl.ds(h, 1), :] = jnp.broadcast_to(
            share * rest * jnp.sum(dshare, axis=0, keepdims=True), (1, width)
        )
        first_col = iota((tok, width), 1) == 0
        pull = jnp.concatenate([rest * a, jnp.where(first_col, -rest * c, 0.0)], axis=1)
        daff = jnp.where(far, mm_lhs(pull, v_near, NT), 0.0)
        dqf = mm(daff, kf, NN) + mm(pull, high[...], NT) + mm(pull, low[...], NT)
        dext[...] += mm(daff, qf, TN)
        dstate[...] += mm(qf, pull, TN)
        dpre = feature_pull(p, n, dqf[:, :width], dqf[:, width:])
        qgrad_ref[h] = mm_rhs(q, dpre, TN)

    student_ref[...] = out_scr[...].reshape(tok, heads, width).astype(BF16)
    teacher_ref[...] = tea_scr[...].reshape(tok, heads, width).astype(BF16)

    kgrad_ref[...] = jnp.zeros_like(kgrad_ref)

    @pl.loop(0, length // chunk)
    def _(c):
        begin = pl.multiple_of(c * chunk, chunk)
        rows = pl.ds(WINDOW + begin, chunk)
        before = (begin + iota((chunk, 1), 0)) < first - WINDOW
        dkf = jnp.where(before, mm_rhs(with_ones(vpad[rows]), dstate[...], NT), 0.0)
        kf = feat[rows]
        dpre = feature_pull(kf[:, :width], kf[:, width:], dkf[:, :width], dkf[:, width:])
        kgrad_ref[group] += mm_rhs(kpad[rows], dpre, TN)

    kf, dkf = feat[near], dext[...]
    dpre = feature_pull(kf[:, :width], kf[:, width:], dkf[:, :width], dkf[:, width:])
    kgrad_ref[group] += mm_rhs(kpad[near], dpre, TN)


def shards(queries, keys, values, query_map, key_map, window_logit):
    tok, heads, width = queries.shape
    count = lax.axis_size("seq")
    group = lax.axis_index("head") * heads // GROUP_HEADS
    own = jnp.stack(
        [
            lax.dynamic_index_in_dim(keys, group, 1, keepdims=False),
            lax.dynamic_index_in_dim(values, group, 1, keepdims=False),
        ]
    )
    kv = lax.all_gather(own, "seq", axis=0)
    length = count * tok
    chunk = tok
    while chunk < 1024 and length % (2 * chunk) == 0:
        chunk *= 2
    vm = pl.BlockSpec(memory_space=pltpu.VMEM)
    student, teacher, qgrad, kgrad, lgrad = pl.pallas_call(
        functools.partial(local_kernel, (count, tok, heads, width, chunk)),
        out_shape=(
            jax.ShapeDtypeStruct((tok, heads, width), BF16),
            jax.ShapeDtypeStruct((tok, heads, width), BF16),
            jax.ShapeDtypeStruct((heads, width, width), F32),
            jax.ShapeDtypeStruct(key_map.shape, F32),
            jax.ShapeDtypeStruct((heads, width), F32),
        ),
        in_specs=[vm, vm, vm, vm, pl.BlockSpec(memory_space=pltpu.SMEM)],
        out_specs=(vm,) * 5,
        scratch_shapes=[
            pltpu.VMEM((tok * heads, width), F32),
            pltpu.VMEM((tok * heads, width), F32),
            pltpu.VMEM((tok * heads, width), F32),
            pltpu.VMEM((length + WINDOW, 2 * width), F32),
            pltpu.VMEM((2 * width, 2 * width), F32),
            pltpu.VMEM((2 * width, 2 * width), F32),
            pltpu.VMEM((tok, 2 * width), F32),
            pltpu.VMEM((length + WINDOW, width), BF16),
            pltpu.VMEM((length + WINDOW, width), BF16),
            pltpu.VMEM((2 * width, 2 * width), BF16),
            pltpu.VMEM((2 * width, 2 * width), BF16),
        ],
        compiler_params=pltpu.CompilerParams(vmem_limit_bytes=56 * 2**20),
    )(queries, kv, query_map, key_map, window_logit)
    qgrad, lgrad = lax.psum((qgrad, lgrad), "seq")
    kgrad = lax.psum(kgrad, ("seq", "head"))
    return student, teacher, qgrad, kgrad, lgrad[:, 0]


def solution(mesh):
    placed = (
        P("seq", "head", None),
        P("seq", None, None),
        P("seq", None, None),
        P("head", None, None),
        P(),
        P("head"),
    )
    return jax.shard_map(
        shards,
        mesh=mesh,
        in_specs=placed,
        out_specs=(
            P("seq", "head", None),
            P("seq", "head", None),
            P("head", None, None),
            P(),
            P("head"),
        ),
        check_vma=False,
    )
```

time: 378 us -> 272 us (0.72)
  blocking collectives: 116 us -> 56.7 us
  matrix products: 31.6 us -> 0 us
  Pallas kernels: 0 us -> 20.2 us
  local copies, waits for them, and re-layouts: 17.3 us -> 4.23 us
  other arithmetic: 13 us -> 0.01 us
  starting transfers between devices: 8.68 us -> 0.08 us
    all_gather x4 -> x1, blocking collectives: 96.7 us -> 35.2 us  [shards(): kv = lax.all_gather(own, 'seq', axis=0)]
    dot_general x26 -> x0, matrix products: 31.6 us -> none  [the longest x3 5.46 us: local_out(): jnp.einsum('htf,kf->htk', query_feats, key_feats, precision=PRECISE)]
    pallas_call x0 -> x1, Pallas kernels: none -> 20.2 us  [shards(): pl.pallas_call(functools.partial(local_kernel, (count, tok, heads, width,...]
    ppermute x2 -> x0, starting transfers between devices: 8.3 us -> none  [shifted(): lax.ppermute(value, axis, [(source, source + steps) for source in range(l...]
    reduce_sum x11 -> x0, other arithmetic: 6.09 us -> none  [the longest x4 2.77 us: hedgehog(): jax.nn.softmax(-preact, axis=-1)]
    dynamic_slice x9 -> x1, local copies, waits for them, and re-layouts: 6.85 us -> 1.02 us  [shards(): lax.dynamic_index_in_dim(values, group, 1, keepdims=False)]
    unnamed x133 -> x8, local copies, waits for them, and re-layouts: 7.86 us -> 2.58 us
    psum x2, waiting for transfers between devices: 172 us -> 176 us  [the longest x1 101 us: shards(): kgrad = lax.psum(kgrad, ('seq', 'head'))]
  transfers between devices with their start and end apart: 6 -> 2, of which waited for: 3 -> 2; matrix products, arithmetic and copies ran while one was open for 12% -> 0% of each run, Pallas kernels for 0% -> 0%
where the time goes in v1:
time: 272 us
  waiting for transfers between devices  177 us (65%)
  blocking collectives  56.7 us (21%)
  Pallas kernels  20.2 us (7%)
  between operations  14.1 us (5%)
  local copies, waits for them, and re-layouts  4.23 us (2%)
    psum x1, waiting for transfers between devices, shards(): kgrad = lax.psum(kgrad, ('seq', 'head'))  101 us
    psum x1, waiting for transfers between devices, shards(): qgrad, lgrad = lax.psum((qgrad, lgrad), 'seq')  75.4 us
    all_gather x1, blocking collectives, shards(): kv = lax.all_gather(own, 'seq', axis=0)  35.2 us
    psum x1, blocking collectives, shards(): qgrad, lgrad = lax.psum((qgrad, lgrad), 'seq')  21.5 us
    pallas_call x1, Pallas kernels, shards(): pl.pallas_call(functools.partial(local_kernel, (count, tok, heads, width,...  20.2 us
  transfers between devices with their start and end apart: 2, of which 2 were waited for; matrix products, arithmetic and copies ran while one was open for 0% of the time, Pallas kernels for 0%

profile of v1, /device:TPU:0, one launch (start us, length us, event | category | flops | bytes accessed | tf_op | source)
XLA Modules:
  0.0 272.1 jit_solution(3030407357975050104)
XLA Ops:
  7.2 0.0 all-reduce.5.cloned.1.call-start
  7.2 1.0 constant_dynamic-slice_fusion
  8.3 35.2 %all-gather = bf16[16,128,128]{2,1,0:T(8,128)(2,1)} all-gather(bf16[2,128,128]{2,1,0:T(8,128)(2,1)S(1)} %pad_maximum_fusion), channel_id=2, replica_groups=mesh['seq'=8,'head'=4] {'seq'}, dimensions={0}, use_global_device_ids=true | all-gather | bytes 589824 | tf_op jit(solution)/shard_map/all_gather | solution.py:177
  43.5 20.2 %shard_map.101 = (bf16[128,8,128]{2,1,0:T(8,128)(2,1)}, bf16[128,8,128]{2,1,0:T(8,128)(2,1)}, f32[8,128,128]{2,1,0:T(8,128)}, f32[2,128,128]{2,1,0:T(8,128)}, f32[8,128]{1,0:T(8,128)}) custom-call(bf16[128,8,128]{2,1,0:T(8,128)(2,1)} %q_ref.1, bf16[8,2,128,128]{3,2,1,0:T(8,128)(2,1)} %bitcast.7, f32[8,128,128]{2,1,0:T(8,128)} %mq_ref.1, ...), custom_call_target="tpu_custom_call" | custom-call | tf_op jit(solution)/shard_map/pallas_call | solution.py:183
  63.7 0.0 all-reduce.5.cloned.1.call-update
  63.7 0.0 all-reduce.3.cloned.1.call-start
  63.8 0.0 copy-start.1
  63.8 0.7 all-reduce.3.cloned.1.call-update
  64.5 0.0 copy-done.1
  64.5 21.5 %psum.23 = f32[8,128]{1,0:T(8,128)S(1)} all-reduce(f32[8,128]{1,0:T(8,128)S(1)} %copy-done.1), channel_id=1, replica_groups=mesh['seq'=8,'head'=4] {'seq'}, use_global_device_ids=true, to_apply=%region_2.3 | all-reduce | flops 1024 | bytes 8192 | tf_op jit(solution)/shard_map/psum | solution.py:209
  85.9 0.6 slice_reduce_fusion
  86.6 100.7 %all-reduce.5.cloned.1.call-done = f32[2,128,128]{2,1,0:T(8,128)} async-done(((f32[2,128,128]{2,1,0:T(8,128)}), f32[2,128,128]{2,1,0:T(8,128)}) %all-reduce.5.cloned.1.call-update) | async-done | bytes 131088 | tf_op jit(solution)/shard_map/psum | solution.py:210
  187.3 75.4 %all-reduce.3.cloned.1.call-done = f32[8,128,128]{2,1,0:T(8,128)} async-done(((f32[8,128,128]{2,1,0:T(8,128)}), f32[8,128,128]{2,1,0:T(8,128)}) %all-reduce.3.cloned.1.call-update) | async-done | bytes 524304 | tf_op jit(solution)/shard_map/psum | solution.py:209
  262.7 0.0 copy-start
  262.7 1.9 copy.23
  264.6 0.0 copy-done
  264.6 0.7 copy.24
  (3 shorter events, 0.0 us)
Async XLA Ops:
  7.2 180.2 %all-reduce.5.cloned.1.call-start = ((), (), s32[]{:S(2)}) async-start(), calls=%async_computation.1 | async-start | bytes 262144 | tf_op jit(solution)/shard_map/psum | solution.py:210
  63.7 199.0 %all-reduce.3.cloned.1.call-start = ((), (), s32[]{:S(2)}) async-start(), calls=%async_computation | async-start | bytes 1048576 | tf_op jit(solution)/shard_map/psum | solution.py:209
  63.8 0.7 copy-start.1
  262.7 1.9 copy-start
Sparse Core Ops, SparseCore 0:
  63.8 123.4 all-reduce.4
  191.3 71.3 all-reduce.2

commit v2 on v1

--- a/solution.py
+++ b/solution.py
@@ -157,11 +157,100 @@
         dkf = jnp.where(before, mm_rhs(with_ones(vpad[rows]), dstate[...], NT), 0.0)
         kf = feat[rows]
         dpre = feature_pull(kf[:, :width], kf[:, width:], dkf[:, :width], dkf[:, width:])
-        kgrad_ref[group] += mm_rhs(kpad[rows], dpre, TN)
+        kgrad_ref[...] += mm_rhs(kpad[rows], dpre, TN)
 
     kf, dkf = feat[near], dext[...]
     dpre = feature_pull(kf[:, :width], kf[:, width:], dkf[:, :width], dkf[:, width:])
-    kgrad_ref[group] += mm_rhs(kpad[near], dpre, TN)
+    kgrad_ref[...] += mm_rhs(kpad[near], dpre, TN)
+
+
+def meet(axes):
+    barrier = pltpu.get_barrier_semaphore()
+    signals = 0
+    for axis in axes:
+        count = lax.axis_size(axis)
+        me = lax.axis_index(axis)
+        for k in range(1, count):
+            pl.semaphore_signal(
+                barrier, inc=1, device_id={axis: lax.rem(me + k, count)},
+                device_id_type=pl.DeviceIdType.MESH,
+            )
+            signals += 1
+    pl.semaphore_wait(barrier, signals)
+
+
+def push(axis, source, slots, send_sem, recv_sem):
+    count = lax.axis_size(axis)
+    me = lax.axis_index(axis)
+    copies = []
+    for k in range(1, count):
+        peer = lax.rem(me + k, count)
+        copy = pltpu.make_async_remote_copy(
+            src_ref=source(peer),
+            dst_ref=slots.at[k - 1],
+            send_sem=send_sem.at[k - 1],
+            recv_sem=recv_sem.at[k - 1],
+            device_id={axis: peer},
+            device_id_type=pl.DeviceIdType.MESH,
+        )
+        copy.start()
+        copies.append(copy)
+    return copies
+
+
+def gather_kernel(own_ref, kv_ref, slots, send_sem, recv_sem):
+    count = lax.axis_size("seq")
+    me = lax.axis_index("seq")
+    meet(("seq",))
+    copies = push("seq", lambda peer: own_ref, slots, send_sem, recv_sem)
+    kv_ref[me] = own_ref[...]
+    for k, copy in enumerate(copies, 1):
+        copy.wait_recv()
+        kv_ref[lax.rem(me + count - k, count)] = slots[k - 1]
+    for copy in copies:
+        copy.wait_send()
+
+
+def reduce_kernel(
+    sizes, q_ref, k_ref, l_ref, qsum_ref, ksum_ref, lsum_ref,
+    pieces, landed, total, parts, own_k, other_k, send1, recv1, send2, recv2, send3, recv3,
+):
+    heads, groups = sizes
+    count, ranks = lax.axis_size("seq"), lax.axis_size("head")
+    me, rank = lax.axis_index("seq"), lax.axis_index("head")
+    q_rows, k_rows, l_rows = q_ref.shape[1], k_ref.shape[1], l_ref.shape[0]
+    q_part = pl.ds(0, q_rows)
+    l_part = pl.ds(q_rows, l_rows)
+    k_part = pl.ds(q_rows + l_rows, k_rows)
+    pieces[:, q_part] = q_ref[...]
+    pieces[:, k_part] = k_ref[...]
+    for piece in range(count):
+        pieces[piece, l_part] = l_ref[...]
+    meet(("seq", "head"))
+    first = push("seq", lambda peer: pieces.at[peer], landed, send1, recv1)
+    summed = pieces[me]
+    for k, copy in enumerate(first):
+        copy.wait_recv()
+        summed = summed + landed[k]
+    total[...] = summed
+    second = push("seq", lambda peer: total, parts, send2, recv2)
+    qsum_ref[me] = total[q_part]
+    own_k[me] = total[k_part]
+    lsum_ref[...] = total[l_part]
+    for k, copy in enumerate(second, 1):
+        copy.wait_recv()
+        origin = lax.rem(me + count - k, count)
+        qsum_ref[origin] = parts[k - 1, q_part]
+        own_k[origin] = parts[k - 1, k_part]
+    third = push("head", lambda peer: own_k, other_k, send3, recv3)
+    ksum_ref[...] = jnp.zeros_like(ksum_ref)
+    ksum_ref[rank * heads // GROUP_HEADS] = own_k[...]
+    for k, copy in enumerate(third, 1):
+        copy.wait_recv()
+        origin = lax.rem(rank + ranks - k, ranks)
+        ksum_ref[origin * heads // GROUP_HEADS] += other_k[k - 1]
+    for copy in first + second + third:
+        copy.wait_send()
 
 
 def shards(queries, keys, values, query_map, key_map, window_logit):
@@ -174,19 +263,33 @@
             lax.dynamic_index_in_dim(values, group, 1, keepdims=False),
         ]
     )
-    kv = lax.all_gather(own, "seq", axis=0)
+    vm = pl.BlockSpec(memory_space=pltpu.VMEM)
+    dma = pltpu.SemaphoreType.DMA
+    kv = pl.pallas_call(
+        gather_kernel,
+        out_shape=jax.ShapeDtypeStruct((count,) + own.shape, BF16),
+        in_specs=[vm],
+        out_specs=vm,
+        scratch_shapes=[
+            pltpu.VMEM((count - 1,) + own.shape, BF16),
+            dma((count - 1,)),
+            dma((count - 1,)),
+        ],
+        compiler_params=pltpu.CompilerParams(
+            collective_id=0, has_side_effects=True, vmem_limit_bytes=40 * 2**20
+        ),
+    )(own)
     length = count * tok
     chunk = tok
     while chunk < 1024 and length % (2 * chunk) == 0:
         chunk *= 2
-    vm = pl.BlockSpec(memory_space=pltpu.VMEM)
     student, teacher, qgrad, kgrad, lgrad = pl.pallas_call(
         functools.partial(local_kernel, (count, tok, heads, width, chunk)),
         out_shape=(
             jax.ShapeDtypeStruct((tok, heads, width), BF16),
             jax.ShapeDtypeStruct((tok, heads, width), BF16),
             jax.ShapeDtypeStruct((heads, width, width), F32),
-            jax.ShapeDtypeStruct(key_map.shape, F32),
+            jax.ShapeDtypeStruct((width, width), F32),
             jax.ShapeDtypeStruct((heads, width), F32),
         ),
         in_specs=[vm, vm, vm, vm, pl.BlockSpec(memory_space=pltpu.SMEM)],
@@ -206,8 +309,42 @@
         ],
         compiler_params=pltpu.CompilerParams(vmem_limit_bytes=56 * 2**20),
     )(queries, kv, query_map, key_map, window_logit)
-    qgrad, lgrad = lax.psum((qgrad, lgrad), "seq")
-    kgrad = lax.psum(kgrad, ("seq", "head"))
+    ranks, groups = lax.axis_size("head"), key_map.shape[0]
+    q_rows, k_rows = heads * width // count, width // count
+    rows = q_rows + heads + k_rows
+    qgrad, kgrad, lgrad = pl.pallas_call(
+        functools.partial(reduce_kernel, (heads, groups)),
+        out_shape=(
+            jax.ShapeDtypeStruct((count, q_rows, width), F32),
+            jax.ShapeDtypeStruct((groups, count, k_rows, width), F32),
+            jax.ShapeDtypeStruct((heads, width), F32),
+        ),
+        in_specs=[vm] * 3,
+        out_specs=(vm,) * 3,
+        scratch_shapes=[
+            pltpu.VMEM((count, rows, width), F32),
+            pltpu.VMEM((count - 1, rows, width), F32),
+            pltpu.VMEM((rows, width), F32),
+            pltpu.VMEM((count - 1, rows, width), F32),
+            pltpu.VMEM((count, k_rows, width), F32),
+            pltpu.VMEM((ranks - 1, count, k_rows, width), F32),
+            dma((count - 1,)),
+            dma((count - 1,)),
+            dma((count - 1,)),
+            dma((count - 1,)),
+            dma((ranks - 1,)),
+            dma((ranks - 1,)),
+        ],
+        compiler_params=pltpu.CompilerParams(
+            collective_id=1, has_side_effects=True, vmem_limit_bytes=40 * 2**20
+        ),
+    )(
+        qgrad.reshape(count, q_rows, width),
+        kgrad.reshape(count, k_rows, width),
+        lgrad,
+    )
+    qgrad = qgrad.reshape(query_map.shape)
+    kgrad = kgrad.reshape(key_map.shape)
     return student, teacher, qgrad, kgrad, lgrad[:, 0]
 
 

time: 272 us -> 79 us (0.29)
  waiting for transfers between devices: 177 us -> 0 us
  blocking collectives: 56.7 us -> 0 us
  Pallas kernels: 20.2 us -> 71.2 us
  between operations: 14.1 us -> 0.71 us
    psum x2 -> x0, waiting for transfers between devices: 176 us -> none  [the longest x1 101 us: shards(): kgrad = lax.psum(kgrad, ('seq', 'head'))]
    pallas_call x0 -> x2, Pallas kernels: none -> 51.1 us  [the longest x1 36.5 us: shards(): pl.pallas_call(functools.partial(reduce_kernel, (heads, groups)), out_sha...]
    all_gather x1 -> x0, blocking collectives: 35.2 us -> none  [shards(): kv = lax.all_gather(own, 'seq', axis=0)]
    psum x1 -> x0, blocking collectives: 21.5 us -> none  [shards(): qgrad, lgrad = lax.psum((qgrad, lgrad), 'seq')]
  transfers between devices with their start and end apart: 2 -> 0, of which waited for: 2 -> 0; matrix products, arithmetic and copies ran while one was open for 0% -> 0% of each run, Pallas kernels for 0% -> 0%
where the time goes in v2:
time: 79 us; the launch traced here: 78.4 us
  Pallas kernels  71.2 us (90%)
  local copies, waits for them, and re-layouts  6.44 us (8%)
    pallas_call x1, Pallas kernels, shards(): pl.pallas_call(functools.partial(reduce_kernel, (heads, groups)), out_sha...  36.5 us
    pallas_call x1, Pallas kernels, shards(): pl.pallas_call(functools.partial(local_kernel, (count, tok, heads, width,...  20.2 us
    pallas_call x1, Pallas kernels, shards(): pl.pallas_call(gather_kernel, out_shape=jax.ShapeDtypeStruct((count,) + o...  14.6 us
    unnamed x12, local copies, waits for them, and re-layouts  4.8 us

profile of v2, /device:TPU:0, one launch (start us, length us, event | category | flops | bytes accessed | tf_op | source)
XLA Modules:
  0.0 78.4 jit_solution(2075886471501757416)
XLA Ops:
  0.7 1.0 %constant_dynamic-slice_fusion = (bf16[128,1,128]{2,1,0:T(2,128)(2,1)S(1)}, bf16[128,1,128]{2,1,0:T(2,128)(2,1)S(1)}) fusion(bf16[128,2,128]{2,1,0:T(2,128)(2,1)} %param.8, s32[]{:T(128)S(6)} %select_n.11, bf16[128,2,128]{2,1,0:T(2,128)(2,1)} %param.7), kind=kLoop, calls=%fused_computation.4 | loop fusion | bytes 131076 | tf_op jit(solution)/shard_map/jit(dynamic_index_in_dim)/dynamic_slice | solution.py:263
  1.7 14.6 %shard_map.101.kv_ref = bf16[8,2,128,128]{3,2,1,0:T(8,128)(2,1)S(1)} custom-call(bf16[2,128,128]{2,1,0:T(8,128)(2,1)S(1)} %pad_maximum_fusion.own_ref), custom_call_target="tpu_custom_call" | custom-call | tf_op jit(solution)/shard_map/pallas_call | solution.py:268
  16.3 0.0 copy-start
  16.3 0.8 copy-done
  17.1 20.2 %shard_map.102 = (bf16[128,8,128]{2,1,0:T(8,128)(2,1)}, bf16[128,8,128]{2,1,0:T(8,128)(2,1)}, f32[8,128,128]{2,1,0:T(8,128)}, f32[128,128]{1,0:T(8,128)}, f32[8,128]{1,0:T(8,128)}) custom-call(bf16[128,8,128]{2,1,0:T(8,128)(2,1)} %q_ref.1, bf16[8,2,128,128]{3,2,1,0:T(8,128)(2,1)} %copy-done, f32[8,128,128]{2,1,0:T(8,128)} %mq_ref.1, f32[2,128,128]{2,1,0:T(8,128)} %mk_ref.1, ...), custom_call_target="tpu_custom_call" | custom-call | tf_op jit(solution)/shard_map/pallas_call | solution.py:286
  37.2 0.0 copy-start.3
  37.2 0.7 copy-done.3
  37.9 0.0 copy-start.1
  37.9 1.0 %copy-done.1 = f32[8,128,128]{2,1,0:T(8,128)S(1)} copy-done((f32[8,128,128]{2,1,0:T(8,128)S(1)}, f32[8,128,128]{2,1,0:T(8,128)}, u32[]{:S(2)}) %copy-start.1) | copy-done | bytes 524312
  39.0 0.0 copy-start.2
  39.0 0.8 %copy-done.2 = f32[128,128]{1,0:T(8,128)S(1)} copy-done((f32[128,128]{1,0:T(8,128)S(1)}, f32[128,128]{1,0:T(8,128)}, u32[]{:S(2)}) %copy-start.2) | copy-done | bytes 65560
  39.8 36.5 %shard_map.103 = (f32[8,128,128]{2,1,0:T(8,128)S(1)}, f32[2,8,16,128]{3,2,1,0:T(8,128)S(1)}, f32[8,128]{1,0:T(8,128)S(1)}) custom-call(f32[8,128,128]{2,1,0:T(8,128)S(1)} %copy-done.1, f32[8,16,128]{2,1,0:T(8,128)S(1)} %bitcast.9, f32[8,128]{1,0:T(8,128)S(1)} %copy-done.3), custom_call_target="tpu_custom_call" | custom-call | tf_op jit(solution)/shard_map/pallas_call | solution.py:315
  76.3 0.6 slice_reduce_fusion
  76.9 0.8 %copy.21 = f32[8,128,128]{2,1,0:T(8,128)} copy(f32[8,128,128]{2,1,0:T(8,128)S(1)} %get-tuple-element.30) | data formatting | bytes 1048576
  77.7 0.7 copy.22
  (3 shorter events, 0.0 us)
Async XLA Ops:
  16.3 0.8 %copy-start = (bf16[8,2,128,128]{3,2,1,0:T(8,128)(2,1)}, bf16[8,2,128,128]{3,2,1,0:T(8,128)(2,1)S(1)}, u32[]{:S(2)}) copy-start(bf16[8,2,128,128]{3,2,1,0:T(8,128)(2,1)S(1)} %shard_map.101.kv_ref) | copy-start | bytes 1572868
  37.2 0.7 copy-start.3
  37.9 1.0 %copy-start.1 = (f32[8,128,128]{2,1,0:T(8,128)S(1)}, f32[8,128,128]{2,1,0:T(8,128)}, u32[]{:S(2)}) copy-start(f32[8,128,128]{2,1,0:T(8,128)} %get-tuple-element.15.q_ref) | copy-start | bytes 1572868
  39.0 0.8 %copy-start.2 = (f32[128,128]{1,0:T(8,128)S(1)}, f32[128,128]{1,0:T(8,128)}, u32[]{:S(2)}) copy-start(f32[128,128]{1,0:T(8,128)} %get-tuple-element.16) | copy-start | bytes 196612

commit v3 on v2

--- a/solution.py
+++ b/solution.py
@@ -220,28 +220,43 @@
     me, rank = lax.axis_index("seq"), lax.axis_index("head")
     q_rows, k_rows, l_rows = q_ref.shape[1], k_ref.shape[1], l_ref.shape[0]
     q_part = pl.ds(0, q_rows)
-    l_part = pl.ds(q_rows, l_rows)
-    k_part = pl.ds(q_rows + l_rows, k_rows)
-    pieces[:, q_part] = q_ref[...]
-    pieces[:, k_part] = k_ref[...]
+    k_part = pl.ds(q_rows + 2 * l_rows, k_rows)
+
+    def logits_of(block):
+        return block[q_rows : q_rows + l_rows] + block[q_rows + l_rows : q_rows + 2 * l_rows]
+
+    pieces[...] = jnp.zeros_like(pieces)
+    pieces[:, q_part] = q_ref[...].astype(BF16)
+    pieces[:, k_part] = k_ref[...].astype(BF16)
+    l_both = jnp.concatenate(split(l_ref[...]), axis=0)
     for piece in range(count):
-        pieces[piece, l_part] = l_ref[...]
+        pieces[piece, pl.ds(q_rows, 2 * l_rows)] = l_both
     meet(("seq", "head"))
     first = push("seq", lambda peer: pieces.at[peer], landed, send1, recv1)
-    summed = pieces[me]
+    q_sum, k_sum = q_ref[me], k_ref[me]
+    l_sum = logits_of(pieces[me].astype(F32))
     for k, copy in enumerate(first):
         copy.wait_recv()
-        summed = summed + landed[k]
-    total[...] = summed
+        block = landed[k].astype(F32)
+        q_sum = q_sum + block[:q_rows]
+        l_sum = l_sum + logits_of(block)
+        k_sum = k_sum + block[q_rows + 2 * l_rows : q_rows + 2 * l_rows + k_rows]
+    total[...] = jnp.zeros_like(total)
+    total[q_part] = q_sum.astype(BF16)
+    total[k_part] = k_sum.astype(BF16)
+    total[pl.ds(q_rows, 2 * l_rows)] = jnp.concatenate(split(l_sum), axis=0)
     second = push("seq", lambda peer: total, parts, send2, recv2)
-    qsum_ref[me] = total[q_part]
-    own_k[me] = total[k_part]
-    lsum_ref[...] = total[l_part]
+    qsum_ref[me] = total[q_part].astype(F32)
+    own_k[me] = total[k_part].astype(F32)
+    mine = logits_of(total[...].astype(F32))
+    lsum_ref[...] = jnp.where(me == 0, mine, 0.0)
     for k, copy in enumerate(second, 1):
         copy.wait_recv()
         origin = lax.rem(me + count - k, count)
-        qsum_ref[origin] = parts[k - 1, q_part]
-        own_k[origin] = parts[k - 1, k_part]
+        block = parts[k - 1].astype(F32)
+        qsum_ref[origin] = block[:q_rows]
+        own_k[origin] = block[q_rows + 2 * l_rows : q_rows + 2 * l_rows + k_rows]
+        lsum_ref[...] += jnp.where(origin == 0, logits_of(block), 0.0)
     third = push("head", lambda peer: own_k, other_k, send3, recv3)
     ksum_ref[...] = jnp.zeros_like(ksum_ref)
     ksum_ref[rank * heads // GROUP_HEADS] = own_k[...]
@@ -311,7 +326,7 @@
     )(queries, kv, query_map, key_map, window_logit)
     ranks, groups = lax.axis_size("head"), key_map.shape[0]
     q_rows, k_rows = heads * width // count, width // count
-    rows = q_rows + heads + k_rows
+    rows = -(-(q_rows + 2 * heads + k_rows) // 16) * 16
     qgrad, kgrad, lgrad = pl.pallas_call(
         functools.partial(reduce_kernel, (heads, groups)),
         out_shape=(
@@ -322,10 +337,10 @@
         in_specs=[vm] * 3,
         out_specs=(vm,) * 3,
         scratch_shapes=[
-            pltpu.VMEM((count, rows, width), F32),
-            pltpu.VMEM((count - 1, rows, width), F32),
-            pltpu.VMEM((rows, width), F32),
-            pltpu.VMEM((count - 1, rows, width), F32),
+            pltpu.VMEM((count, rows, width), BF16),
+            pltpu.VMEM((count - 1, rows, width), BF16),
+            pltpu.VMEM((rows, width), BF16),
+            pltpu.VMEM((count - 1, rows, width), BF16),
             pltpu.VMEM((count, k_rows, width), F32),
             pltpu.VMEM((ranks - 1, count, k_rows, width), F32),
             dma((count - 1,)),

time: 79 us -> 67.4 us (0.85)
  Pallas kernels: 71.2 us -> 59.8 us
    pallas_call x1, Pallas kernels: 36.5 us -> 25.1 us  [shards(): pl.pallas_call(functools.partial(reduce_kernel, (heads, groups)), out_sha...]
where the time goes in v3:
time: 67.4 us; the launch traced here: 67 us
  Pallas kernels  59.8 us (89%)
  local copies, waits for them, and re-layouts  6.44 us (10%)
  between operations  0.71 us (1%)
    pallas_call x1, Pallas kernels, shards(): pl.pallas_call(functools.partial(reduce_kernel, (heads, groups)), out_sha...  25.1 us
    pallas_call x1, Pallas kernels, shards(): pl.pallas_call(functools.partial(local_kernel, (count, tok, heads, width,...  20.2 us
    pallas_call x1, Pallas kernels, shards(): pl.pallas_call(gather_kernel, out_shape=jax.ShapeDtypeStruct((count,) + o...  14.6 us
    unnamed x12, local copies, waits for them, and re-layouts  4.8 us

profile of v3, /device:TPU:0, one launch (start us, length us, event | category | flops | bytes accessed | tf_op | source)
XLA Modules:
  0.0 67.0 jit_solution(1279291671187110887)
XLA Ops:
  0.7 1.0 %constant_dynamic-slice_fusion = (bf16[128,1,128]{2,1,0:T(2,128)(2,1)S(1)}, bf16[128,1,128]{2,1,0:T(2,128)(2,1)S(1)}) fusion(bf16[128,2,128]{2,1,0:T(2,128)(2,1)} %param.8, s32[]{:T(128)S(6)} %select_n.11, bf16[128,2,128]{2,1,0:T(2,128)(2,1)} %param.7), kind=kLoop, calls=%fused_computation.4 | loop fusion | bytes 131076 | tf_op jit(solution)/shard_map/jit(dynamic_index_in_dim)/dynamic_slice | solution.py:278
  1.7 14.6 %shard_map.101.kv_ref = bf16[8,2,128,128]{3,2,1,0:T(8,128)(2,1)S(1)} custom-call(bf16[2,128,128]{2,1,0:T(8,128)(2,1)S(1)} %pad_maximum_fusion.own_ref), custom_call_target="tpu_custom_call" | custom-call | tf_op jit(solution)/shard_map/pallas_call | solution.py:283
  16.3 0.0 copy-start
  16.3 0.8 %copy-done = bf16[8,2,128,128]{3,2,1,0:T(8,128)(2,1)} copy-done((bf16[8,2,128,128]{3,2,1,0:T(8,128)(2,1)}, bf16[8,2,128,128]{3,2,1,0:T(8,128)(2,1)S(1)}, u32[]{:S(2)}) %copy-start) | copy-done | bytes 524312
  17.1 20.2 %shard_map.102 = (bf16[128,8,128]{2,1,0:T(8,128)(2,1)}, bf16[128,8,128]{2,1,0:T(8,128)(2,1)}, f32[8,128,128]{2,1,0:T(8,128)}, f32[128,128]{1,0:T(8,128)}, f32[8,128]{1,0:T(8,128)}) custom-call(bf16[128,8,128]{2,1,0:T(8,128)(2,1)} %q_ref.1, bf16[8,2,128,128]{3,2,1,0:T(8,128)(2,1)} %copy-done, f32[8,128,128]{2,1,0:T(8,128)} %mq_ref.1, f32[2,128,128]{2,1,0:T(8,128)} %mk_ref.1, ...), custom_call_target="tpu_custom_call" | custom-call | tf_op jit(solution)/shard_map/pallas_call | solution.py:301
  37.2 0.0 copy-start.3
  37.2 0.7 %copy-done.3 = f32[8,128]{1,0:T(8,128)S(1)} copy-done((f32[8,128]{1,0:T(8,128)S(1)}, f32[8,128]{1,0:T(8,128)}, u32[]{:S(2)}) %copy-start.3) | copy-done | bytes 4120
  37.9 0.0 copy-start.1
  37.9 1.0 %copy-done.1 = f32[8,128,128]{2,1,0:T(8,128)S(1)} copy-done((f32[8,128,128]{2,1,0:T(8,128)S(1)}, f32[8,128,128]{2,1,0:T(8,128)}, u32[]{:S(2)}) %copy-start.1) | copy-done | bytes 524312
  39.0 0.0 copy-start.2
  39.0 0.8 %copy-done.2 = f32[128,128]{1,0:T(8,128)S(1)} copy-done((f32[128,128]{1,0:T(8,128)S(1)}, f32[128,128]{1,0:T(8,128)}, u32[]{:S(2)}) %copy-start.2) | copy-done | bytes 65560
  39.8 25.1 %shard_map.103 = (f32[8,128,128]{2,1,0:T(8,128)S(1)}, f32[2,8,16,128]{3,2,1,0:T(8,128)S(1)}, f32[8,128]{1,0:T(8,128)S(1)}) custom-call(f32[8,128,128]{2,1,0:T(8,128)S(1)} %copy-done.1, f32[8,16,128]{2,1,0:T(8,128)S(1)} %bitcast.9, f32[8,128]{1,0:T(8,128)S(1)} %copy-done.3), custom_call_target="tpu_custom_call" | custom-call | tf_op jit(solution)/shard_map/pallas_call | solution.py:330
  64.9 0.6 slice_reduce_fusion
  65.6 0.8 %copy.21 = f32[8,128,128]{2,1,0:T(8,128)} copy(f32[8,128,128]{2,1,0:T(8,128)S(1)} %get-tuple-element.30) | data formatting | bytes 1048576
  66.3 0.7 copy.22
  (3 shorter events, 0.0 us)
Async XLA Ops:
  16.3 0.8 %copy-start = (bf16[8,2,128,128]{3,2,1,0:T(8,128)(2,1)}, bf16[8,2,128,128]{3,2,1,0:T(8,128)(2,1)S(1)}, u32[]{:S(2)}) copy-start(bf16[8,2,128,128]{3,2,1,0:T(8,128)(2,1)S(1)} %shard_map.101.kv_ref) | copy-start | bytes 1572868
  37.2 0.7 %copy-start.3 = (f32[8,128]{1,0:T(8,128)S(1)}, f32[8,128]{1,0:T(8,128)}, u32[]{:S(2)}) copy-start(f32[8,128]{1,0:T(8,128)} %get-tuple-element.17.l_ref) | copy-start | bytes 12292
  37.9 1.0 %copy-start.1 = (f32[8,128,128]{2,1,0:T(8,128)S(1)}, f32[8,128,128]{2,1,0:T(8,128)}, u32[]{:S(2)}) copy-start(f32[8,128,128]{2,1,0:T(8,128)} %get-tuple-element.15.q_ref) | copy-start | bytes 1572868
  39.0 0.8 %copy-start.2 = (f32[128,128]{1,0:T(8,128)S(1)}, f32[128,128]{1,0:T(8,128)}, u32[]{:S(2)}) copy-start(f32[128,128]{1,0:T(8,128)} %get-tuple-element.16) | copy-start | bytes 196612
